TPU v7x, 32 devices: a whole 2x2x4 slice. The times are simulated.
32 devices in a mesh: seq: 16 (over z, x, core), tp: 2 (over y).
Axes of the slice: x: 2, y: 2, z: 4, core: 2. Of those that a mesh axis runs over, the one named last changes fastest.
Arguments:
- latents: bfloat16 [4096, 3072], P('seq', 'tp'), may hold values from -16 to 16
- noise: bfloat16 [4096, 3072], P('seq', 'tp'), may hold values from -16 to 16
- timestep: int32 [1], replicated, may hold values from 1 to 1000
- text_len: int32 [1], replicated, may hold values from 64 to 256
- text_kv: bfloat16 [2, 256, 3072], P(None, None, 'tp'), may hold values from -32 to 32
- norm_gain: float32 [3072], replicated, may hold values from 0.1 to 1.9
- w_qkv: bfloat16 [3072, 3, 3072], P(None, None, 'tp')
- qk_gain: float32 [2, 128], replicated, may hold values from 0.1 to 1.9
- w_out: bfloat16 [3072, 3072], P('tp'), may hold values from -3 to 3
- out_gate: float32 [3072], P('tp'), may hold values from 0.5 to 1.5
Outputs:
- prediction: bfloat16 [4096, 3072], P('seq', 'tp')
- loss: float32 [], replicated
All inputs are finite; a program needn't handle non-finite values.
Results may differ from a plain program's by a relative error of at most 0.014.
Values may be sent and summed in bfloat16 or wider, within the bound.
A program may use at most 192 MiB of HBM per device.

v0:
```python
import jax
import jax.numpy as jnp
from jax import lax
from jax.sharding import PartitionSpec as P

D = 3072
HD = 128
TXT = 256


def online_block(carry, query, keys, values, valid):
    top, total, accum = carry
    scores = jnp.einsum("rhd,nhd->hrn", query, keys, preferred_element_type=jnp.float32)
    scores = scores / jnp.sqrt(jnp.float32(query.shape[2]))
    if valid is not None:
        scores = jnp.where(valid[None, None, :], scores, -1e30)
    new_top = jnp.maximum(top, jnp.max(scores, axis=-1))
    decay = jnp.exp(top - new_top)
    probs = jnp.exp(scores - new_top[:, :, None])
    total = total * decay + jnp.sum(probs, axis=-1)
    accum = accum * decay[:, :, None] + jnp.einsum(
        "hrn,nhd->hrd", probs.astype(jnp.bfloat16), values, preferred_element_type=jnp.float32
    )
    return (new_top, total, accum)


def shards(latents, noise, timestep, text_len, text_kv, norm_gain, w_qkv, qk_gain, w_out, out_gate):
    rows = latents.shape[0]
    local_width = latents.shape[1]
    sigma = timestep[0].astype(jnp.float32) / 1000.0
    noisy = (1.0 - sigma) * latents.astype(jnp.float32) + sigma * noise.astype(jnp.float32)
    both = (
        lax.all_gather(latents, "tp", axis=1, tiled=True),
        lax.all_gather(noise, "tp", axis=1, tiled=True),
    )
    full = (1.0 - sigma) * both[0].astype(jnp.float32) + sigma * both[1].astype(jnp.float32)
    center = full - jnp.mean(full, axis=-1, keepdims=True)
    spread = jnp.mean(center * center, axis=-1, keepdims=True)
    normed = (center * lax.rsqrt(spread + 1e-06) * norm_gain).astype(jnp.bfloat16)
    head_width = w_qkv.shape[2]
    heads_dev = head_width // HD
    qkv = jnp.dot(normed, w_qkv.reshape(D, 3 * head_width), preferred_element_type=jnp.float32)
    qkv = qkv.reshape(rows, 3, heads_dev, HD)

    def qknorm(block, gain):
        return (
            block * lax.rsqrt(jnp.mean(block * block, axis=-1, keepdims=True) + 1e-06) * gain
        ).astype(jnp.bfloat16)

    query = qknorm(qkv[:, 0], qk_gain[0])
    key = qknorm(qkv[:, 1], qk_gain[1])
    value = qkv[:, 2].astype(jnp.bfloat16)
    start_carry = (
        jnp.full((heads_dev, rows), -1e30, jnp.float32),
        jnp.zeros((heads_dev, rows), jnp.float32),
        jnp.zeros((heads_dev, rows, HD), jnp.float32),
    )
    text_valid = jnp.arange(TXT, dtype=jnp.int32) < text_len[0]
    carry = online_block(
        start_carry,
        query,
        text_kv[0].reshape(TXT, heads_dev, HD),
        text_kv[1].reshape(TXT, heads_dev, HD),
        text_valid,
    )
    paired = jnp.stack([key.reshape(rows, head_width), value.reshape(rows, head_width)], 0)
    gathered = lax.all_gather(paired, "seq", axis=1, tiled=True)
    count = gathered.shape[1]
    size = 1024

    def one_block(index, inner):
        block = lax.dynamic_slice_in_dim(gathered, index * size, size, 1)
        return online_block(
            inner,
            query,
            block[0].reshape(size, heads_dev, HD),
            block[1].reshape(size, heads_dev, HD),
            None,
        )

    carry = lax.fori_loop(0, count // size, one_block, carry)
    top, total, accum = carry
    attended = (accum / total[:, :, None]).astype(jnp.bfloat16)
    attended = jnp.transpose(attended, (1, 0, 2)).reshape(rows, head_width)
    mixed = (
        lax.psum_scatter(
            lax.dot_general(
                w_out, attended, (((0,), (1,)), ((), ())), preferred_element_type=jnp.float32
            ).astype(jnp.bfloat16),
            "tp",
            scatter_dimension=0,
            tiled=True,
        )
        .astype(jnp.float32)
        .T
    )
    prediction = (noisy + out_gate * mixed).astype(jnp.bfloat16)
    target = noise.astype(jnp.float32) - latents.astype(jnp.float32)
    error = prediction.astype(jnp.float32) - target
    total_error = lax.psum(jnp.sum(error * error), ("seq", "tp"))
    count_all = rows * lax.axis_size("seq") * local_width * lax.axis_size("tp")
    loss = total_error / jnp.float32(count_all)
    return (prediction, loss)


def solution(mesh):
    placed = (
        P("seq", "tp"),
        P("seq", "tp"),
        P(),
        P(),
        P(None, None, "tp"),
        P(),
        P(None, None, "tp"),
        P(),
        P("tp", None),
        P("tp"),
    )
    return jax.shard_map(
        shards, mesh=mesh, in_specs=placed, out_specs=(P("seq", "tp"), P()), check_vma=False
    )
```

profile of v0, /device:TPU:0, one launch (start us, length us, event | category | flops | bytes accessed | tf_op | source)
XLA Modules:
  0.0 378.6 jit_solution(15404121701311360497)
XLA Ops:
  9.3 36.8 %copy.22 = bf16[3072,3,1536]{0,2,1:T(8,128)(2,1)} copy(bf16[3072,3,1536]{2,0,1:T(8,128)(2,1)} %param.18) | data formatting | bytes 56623104 | tf_op args[6]
  46.2 22.1 %all-gather.6.cloned.1.call-done = bf16[256,3072]{1,0:T(8,128)(2,1)} async-done(((bf16[256,1536]{1,0:T(8,128)(2,1)}), bf16[256,3072]{1,0:T(8,128)(2,1)}) %all-gather.6.cloned.1.call-update) | async-done | bytes 1572880 | tf_op jit(solution)/shard_map/all_gather | solution.py:34
  68.3 2.7 fusion.14
  71.9 13.4 %fusion.24 = f32[256,3,12,128]{0,3,2,1:T(8,128)S(1)} fusion(bf16[3,12,128,3072]{3,2,1,0:T(8,128)(2,1)} %bitcast.85, bf16[256,3072]{1,0:T(8,128)(2,1)S(1)} %copy-done.4, bf16[256,3072]{1,0:T(8,128)(2,1)S(1)} %copy-done.3, f32[3072]{0:T(1024)S(1)} %copy-done.11, f32[256]{0:T(256)S(1)} %add_rsqrt_fusion.2, f32[256]{0:T(256)S(1)} %broadcast_multiply_fusion, ...), kind=kOutput, calls=%fused_computation.36 | convolution fusion | flops 7254835200 | bytes 36190216 | tf_op jit(solution)/shard_map/dot_general | solution.py:42
  98.5 127.3 %all-gather.8.cloned.1.call-done = bf16[2,4096,1536]{1,2,0:T(8,128)(2,1)} async-done(((bf16[2,256,1536]{1,2,0:T(8,128)(2,1)}), bf16[2,4096,1536]{1,2,0:T(8,128)(2,1)}) %all-gather.8.cloned.1.call-update) | async-done | bytes 25165840 | tf_op jit(solution)/shard_map/all_gather | solution.py:67
  225.8 65.7 %while.17 = (s32[]{:T(128)}, f32[12,256]{1,0:T(8,128)S(1)}, f32[12,256]{1,0:T(8,128)S(1)}, f32[12,256,128]{2,1,0:T(8,128)S(1)}, bf16[2,4096,1536]{1,2,0:T(8,128)...) while((s32[]{:T(128)}, f32[12,256]{1,0:T(8,128)S(1)}, ...), condition=%wide.region_9.10_spmd, body=%wide.region_6.9_spmd.sunk | while | flops 1636571136 | bytes 114229480 | solution.py:81
  225.9 3.6 constant_dynamic-slice_fusion.3
  231.4 2.1 fusion.63
  233.4 2.5 copy-done
  236.0 6.3 %multiply_add_fusion.6 = f32[12,256,128]{2,1,0:T(8,128)S(1)} fusion(f32[12,256,128]{2,1,0:T(8,128)S(1)} %get-tuple-element.219, bf16[1024,12,128]{0,2,1:T(8,128)(2,1)S(1)} %bitcast.83, f32[12,1024,256]{2,1,0:T(8,128)} %copy-done, f32[12,256]{1,0:T(8,128)S(1)} %max.8, f32[12,256]{1,0:T(8,128)S(1)} %get-tuple-element.204), kind=kOutput, calls=%fused_computation.8.clone.1 | convolution fusion | flops 815529984 | bytes 18898944 | tf_op jit(solution)/shard_map/while/body/eval_jaxpr/hrn,nhd->hrd/dot_general | solution.py:21
  242.3 3.6 constant_dynamic-slice_fusion.3
  247.8 2.1 fusion.63
  249.9 2.5 copy-done
  252.4 6.3 %multiply_add_fusion.6 = f32[12,256,128]{2,1,0:T(8,128)S(1)} fusion(f32[12,256,128]{2,1,0:T(8,128)S(1)} %get-tuple-element.219, bf16[1024,12,128]{0,2,1:T(8,128)(2,1)S(1)} %bitcast.83, f32[12,1024,256]{2,1,0:T(8,128)} %copy-done, f32[12,256]{1,0:T(8,128)S(1)} %max.8, f32[12,256]{1,0:T(8,128)S(1)} %get-tuple-element.204), kind=kOutput, calls=%fused_computation.8.clone.1 | convolution fusion | flops 815529984 | bytes 18898944 | tf_op jit(solution)/shard_map/while/body/eval_jaxpr/hrn,nhd->hrd/dot_general | solution.py:21
  258.7 3.6 constant_dynamic-slice_fusion.3
  266.3 2.5 copy-done
  268.8 6.3 %multiply_add_fusion.6 = f32[12,256,128]{2,1,0:T(8,128)S(1)} fusion(f32[12,256,128]{2,1,0:T(8,128)S(1)} %get-tuple-element.219, bf16[1024,12,128]{0,2,1:T(8,128)(2,1)S(1)} %bitcast.83, f32[12,1024,256]{2,1,0:T(8,128)} %copy-done, f32[12,256]{1,0:T(8,128)S(1)} %max.8, f32[12,256]{1,0:T(8,128)S(1)} %get-tuple-element.204), kind=kOutput, calls=%fused_computation.8.clone.1 | convolution fusion | flops 815529984 | bytes 18898944 | tf_op jit(solution)/shard_map/while/body/eval_jaxpr/hrn,nhd->hrd/dot_general | solution.py:21
  275.2 3.6 constant_dynamic-slice_fusion.3
  282.8 2.5 copy-done
  285.3 6.3 %multiply_add_fusion.6 = f32[12,256,128]{2,1,0:T(8,128)S(1)} fusion(f32[12,256,128]{2,1,0:T(8,128)S(1)} %get-tuple-element.219, bf16[1024,12,128]{0,2,1:T(8,128)(2,1)S(1)} %bitcast.83, f32[12,1024,256]{2,1,0:T(8,128)} %copy-done, f32[12,256]{1,0:T(8,128)S(1)} %max.8, f32[12,256]{1,0:T(8,128)S(1)} %get-tuple-element.204), kind=kOutput, calls=%fused_computation.8.clone.1 | convolution fusion | flops 815529984 | bytes 18898944 | tf_op jit(solution)/shard_map/while/body/eval_jaxpr/hrn,nhd->hrd/dot_general | solution.py:21
  294.8 7.6 %fusion.10 = bf16[3072,256]{0,1:T(8,128)(2,1)} fusion(bf16[256,1536]{0,1:T(8,128)(2,1)S(1)} %bitcast.86, bf16[1536,3072]{1,0:T(8,128)(2,1)} %param.20), kind=kOutput, calls=%fused_computation.15 | convolution fusion | flops 2416705536 | bytes 11796480 | tf_op jit(solution)/shard_map/dot_general | solution.py:87
  302.4 25.1 %reduce-scatter.2.cloned.1.call-done = bf16[1536,256]{0,1:T(8,128)(2,1)} async-done(((bf16[3072,256]{0,1:T(8,128)(2,1)}), bf16[1536,256]{0,1:T(8,128)(2,1)}) %reduce-scatter.2.cloned.1.call-update) | async-done | bytes 786448 | tf_op jit(solution)/shard_map/reduce_scatter | solution.py:86
  327.5 3.2 fusion.20
  330.8 39.5 %psum.7 = f32[]{:T(128)} all-reduce(f32[]{:T(128)} %get-tuple-element.140), channel_id=1, replica_groups=mesh['seq'=16,'tp'=2] {'seq','tp'}, use_global_device_ids=true, to_apply=%region_12.13 | all-reduce | flops 1 | bytes 8 | tf_op jit(solution)/shard_map/psum | solution.py:100
  (84 shorter events, 29.7 us)
Async XLA Ops:
  7.2 39.0 %all-gather.4.cloned.1.call-start = ((), (), s32[]{:S(2)}) async-start(), calls=%async_computation.1 | async-start | bytes 2359296 | tf_op jit(solution)/shard_map/all_gather | solution.py:33
  7.9 60.4 %all-gather.6.cloned.1.call-start = ((), (), s32[]{:S(2)}) async-start(), calls=%async_computation.2 | async-start | bytes 2359296 | tf_op jit(solution)/shard_map/all_gather | solution.py:34
  8.6 217.2 %all-gather.8.cloned.1.call-start = ((), (), s32[]{:S(2)}) async-start(), calls=%async_computation.3 | async-start | bytes 26738688 | tf_op jit(solution)/shard_map/all_gather | solution.py:67
  9.3 36.8 %copy-start.10 = (f32[2,128]{1,0:T(2,128)S(1)}, f32[2,128]{1,0:T(2,128)}, u32[]{:S(2)}) copy-start(f32[2,128]{1,0:T(2,128)} %param.19) | copy-start | bytes 3076
  46.1 25.8 %copy-start.11 = (f32[3072]{0:T(1024)S(1)}, f32[3072]{0:T(1024)}, u32[]{:S(2)}) copy-start(f32[3072]{0:T(1024)} %param.17) | copy-start | bytes 36868
  46.2 24.8 %copy-start.3 = (bf16[256,3072]{1,0:T(8,128)(2,1)S(1)}, bf16[256,3072]{1,0:T(8,128)(2,1)}, u32[]{:S(2)}) copy-start(bf16[256,3072]{1,0:T(8,128)(2,1)} %all-gather.4.cloned.1.call-done) | copy-start | bytes 4718596
  68.3 2.7 copy-start.4
  85.3 2.2 copy-start.2
  85.7 3.8 copy-start.7
  88.8 238.7 %reduce-scatter.2.cloned.1.call-start = ((), (), s32[]{:S(2)}) async-start(), calls=%async_computation.4 | async-start | bytes 2359296 | tf_op jit(solution)/shard_map/reduce_scatter | solution.py:86
  95.5 1.6 copy-start.8
  225.9 3.6 copy-start.1
  231.4 4.6 %copy-start = (f32[12,1024,256]{2,1,0:T(8,128)}, f32[12,1024,256]{2,1,0:T(8,128)S(1)}, u32[]{:S(2)}) copy-start(f32[12,1024,256]{2,1,0:T(8,128)S(1)} %get-tuple-element.201) | copy-start | bytes 37748740 | tf_op jit(solution)/shard_map/while
  242.3 3.7 copy-start.1
  247.8 4.6 %copy-start = (f32[12,1024,256]{2,1,0:T(8,128)}, f32[12,1024,256]{2,1,0:T(8,128)S(1)}, u32[]{:S(2)}) copy-start(f32[12,1024,256]{2,1,0:T(8,128)S(1)} %get-tuple-element.201) | copy-start | bytes 37748740 | tf_op jit(solution)/shard_map/while
  258.7 3.7 copy-start.1
  264.2 4.6 %copy-start = (f32[12,1024,256]{2,1,0:T(8,128)}, f32[12,1024,256]{2,1,0:T(8,128)S(1)}, u32[]{:S(2)}) copy-start(f32[12,1024,256]{2,1,0:T(8,128)S(1)} %get-tuple-element.201) | copy-start | bytes 37748740 | tf_op jit(solution)/shard_map/while
  275.2 3.7 copy-start.1
  280.7 4.6 %copy-start = (f32[12,1024,256]{2,1,0:T(8,128)}, f32[12,1024,256]{2,1,0:T(8,128)S(1)}, u32[]{:S(2)}) copy-start(f32[12,1024,256]{2,1,0:T(8,128)S(1)} %get-tuple-element.201) | copy-start | bytes 37748740 | tf_op jit(solution)/shard_map/while
  294.8 32.8 %copy-start.5 = (bf16[256,1536]{1,0:T(8,128)(2,1)S(1)}, bf16[256,1536]{1,0:T(8,128)(2,1)}, u32[]{:S(2)}) copy-start(bf16[256,1536]{1,0:T(8,128)(2,1)} %param.12) | copy-start | bytes 2359300
  294.8 32.7 %copy-start.6 = (bf16[256,1536]{1,0:T(8,128)(2,1)S(1)}, bf16[256,1536]{1,0:T(8,128)(2,1)}, u32[]{:S(2)}) copy-start(bf16[256,1536]{1,0:T(8,128)(2,1)} %param.13) | copy-start | bytes 2359300
  294.8 32.7 %copy-start.9 = (f32[1536]{0:T(1024)S(1)}, f32[1536]{0:T(1024)}, u32[]{:S(2)}) copy-start(f32[1536]{0:T(1024)} %param.21) | copy-start | bytes 18436
Sparse Core Ops, SparseCore 0:
  9.5 29.8 all-gather.3
  41.0 27.2 all-gather.5
  88.9 136.8 all-gather.7
  302.5 24.9 reduce-scatter.1
where the time goes:
time: 380 us; the launch traced here: 379 us
  waiting for transfers between devices  176 us (46%)
  local copies, waits for them, and re-layouts  67.2 us (18%)
  matrix products  55.7 us (15%)
  blocking collectives  39.5 us (10%)
  other arithmetic  22.5 us (6%)
  between operations  17.1 us (5%)
    all_gather x1, waiting for transfers between devices, shards(): gathered = lax.all_gather(paired, 'seq', axis=1, tiled=True)  127 us
    unnamed x23, local copies, waits for them, and re-layouts  39.7 us
    psum x1, blocking collectives, shards(): total_error = lax.psum(jnp.sum(error * error), ('seq', 'tp'))  39.5 us
    dot_general x5, matrix products, online_block(): jnp.einsum('hrn,nhd->hrd', probs.astype(jnp.bfloat16), values, preferred_...  26.5 us
    reduce_scatter x1, waiting for transfers between devices, shards(): lax.psum_scatter(lax.dot_general(w_out, attended, (((0,), (1,)), ((), ())...  25.1 us
    all_gather x1, waiting for transfers between devices, shards(): lax.all_gather(noise, 'tp', axis=1, tiled=True)  22.1 us
    slice x4, local copies, waits for them, and re-layouts, one_block(): block[1].reshape(size, heads_dev, HD)  14.5 us
    dot_general x1, matrix products, shards(): jnp.dot(normed, w_qkv.reshape(D, 3 * head_width), preferred_element_type=...  13.4 us
  transfers between devices with their start and end apart: 4, of which 3 were waited for; matrix products, arithmetic and copies ran while one was open for 12% of the time, Pallas kernels for 0%

commit v1 on v0

v1 whole, which is shorter than its diff:
```python
import functools

import jax
import jax.numpy as jnp
from jax import lax
from jax.experimental import pallas as pl
from jax.experimental.pallas import tpu as pltpu
from jax.sharding import PartitionSpec as P

HD = 128
MESH = pl.DeviceIdType.MESH
ANY = pl.BlockSpec(memory_space=pl.ANY)
LOG2E = 1.4426950408889634


def project_kernel(x_ref, w_ref, gain_ref, out_ref):
    part = pl.program_id(0)
    y = jnp.dot(x_ref[...], w_ref[0], preferred_element_type=jnp.float32)
    gain = gain_ref[0]
    for h in range(y.shape[1] // HD):
        block = y[:, h * HD : (h + 1) * HD]
        scale = lax.rsqrt(jnp.mean(block * block, axis=-1, keepdims=True) + 1e-06)
        scale = jnp.where(part < 2, scale, 1.0)
        out_ref[0, 0, :, h * HD : (h + 1) * HD] = (block * scale * gain).astype(jnp.bfloat16)


def project(normed, w, gains, groups):
    rows, depth = normed.shape
    width = w.shape[2] // groups
    return pl.pallas_call(
        project_kernel,
        grid=(3, groups),
        in_specs=[
            pl.BlockSpec((rows, depth), lambda s, g: (0, 0)),
            pl.BlockSpec((1, depth, width), lambda s, g: (s, 0, g)),
            pl.BlockSpec((1, 1, HD), lambda s, g: (s, 0, 0)),
        ],
        out_specs=pl.BlockSpec((1, 1, rows, width), lambda s, g: (s, g, 0, 0)),
        out_shape=jax.ShapeDtypeStruct((3, groups, rows, width), jnp.bfloat16),
        compiler_params=pltpu.CompilerParams(vmem_limit_bytes=40 << 20),
    )(normed, w, gains)


def greet(peers):
    barrier = pltpu.get_barrier_semaphore()
    for peer in peers:
        pl.semaphore_signal(barrier, inc=1, device_id={"seq": peer}, device_id_type=MESH)
    pl.semaphore_wait(barrier, len(peers))


def remote(src, dst, send, recv, peer):
    return pltpu.make_async_remote_copy(
        src_ref=src, dst_ref=dst, send_sem=send, recv_sem=recv,
        device_id={"seq": peer}, device_id_type=MESH,
    )


def deal_kernel(groups, inner, qkv, q_all, kv_all, zs, zr, qs, qr, xs, xr, cs, cr, fs, fr, ls):
    me = lax.axis_index("seq")
    j = lax.rem(me, inner)
    z = me // inner
    core = lax.rem(j, 2)
    x = j // 2
    xj = (1 - x) * 2 + core
    cj = x * 2 + (1 - core)
    x_mate = z * inner + xj
    c_mate = z * inner + cj
    order = [2, 1, 3]
    peers = {k: lax.rem(z + k, groups) * inner + j for k in order}
    greet([peers[k] for k in order] + [x_mate, c_mate])
    waits = []
    firsts = {}
    for k in order:
        to = lax.rem(z + k, groups)
        firsts[k] = remote(
            qkv.at[pl.ds(1, 2), to], kv_all.at[:, z, j], zs.at[k - 1], zr.at[k - 1], peers[k]
        )
        firsts[k].start()
    own_kv = pltpu.make_async_copy(qkv.at[pl.ds(1, 2), z], kv_all.at[:, z, j], ls.at[0])
    own_q = pltpu.make_async_copy(qkv.at[0, z], q_all.at[z], ls.at[1])
    own_kv.start()
    own_q.start()
    by_x = {}
    by_c = {}
    quers = {}
    for k in [0] + order:
        at = lax.rem(z + groups - k, groups)
        if k == 0:
            src = qkv.at[pl.ds(1, 2), z]
        else:
            firsts[k].wait_recv()
            src = kv_all.at[:, at, j]
        by_x[k] = remote(src, kv_all.at[:, at, j], xs.at[k], xr.at[k], x_mate)
        by_x[k].start()
        by_c[k] = remote(src, kv_all.at[:, at, j], cs.at[k], cr.at[k], c_mate)
        by_c[k].start()
        if k == 0:
            for m in order:
                to = lax.rem(z + m, groups)
                quers[m] = remote(
                    qkv.at[0, to], q_all.at[z], qs.at[m - 1], qr.at[m - 1], peers[m]
                )
                quers[m].start()
    passed = {}
    for k in [0] + order:
        at = lax.rem(z + groups - k, groups)
        by_x[k].wait_recv()
        passed[k] = remote(
            kv_all.at[:, at, xj], kv_all.at[:, at, xj], fs.at[k], fr.at[k], c_mate
        )
        passed[k].start()
    own_kv.wait()
    own_q.wait()
    for k in order:
        firsts[k].wait_send()
        quers[k].wait()
    for k in [0] + order:
        by_x[k].wait_send()
        by_c[k].wait()
        passed[k].wait()


def deal(qkv, inner):
    _, groups, rows, width = qkv.shape
    dma = pltpu.SemaphoreType.DMA
    return pl.pallas_call(
        functools.partial(deal_kernel, groups, inner),
        in_specs=[ANY],
        out_specs=[ANY, ANY],
        out_shape=[
            jax.ShapeDtypeStruct((groups, rows, width), jnp.bfloat16),
            jax.ShapeDtypeStruct((2, groups, inner, rows, width), jnp.bfloat16),
        ],
        scratch_shapes=[dma((3,)), dma((3,)), dma((3,)), dma((3,))]
        + [dma((4,)) for _ in range(6)]
        + [dma((2,))],
        compiler_params=pltpu.CompilerParams(collective_id=1, has_side_effects=True),
    )(qkv)


def back_kernel(groups, inner, o_ref, out_ref, ss, rs, ls):
    me = lax.axis_index("seq")
    j = lax.rem(me, inner)
    z = me // inner
    order = [2, 1, 3]
    peers = {k: lax.rem(z + k, groups) * inner + j for k in order}
    greet([peers[k] for k in order])
    copies = []
    for k in order:
        to = lax.rem(z + k, groups)
        copies.append(
            remote(o_ref.at[to], out_ref.at[z], ss.at[k - 1], rs.at[k - 1], peers[k])
        )
        copies[-1].start()
    own = pltpu.make_async_copy(o_ref.at[z], out_ref.at[z], ls.at[0])
    own.start()
    own.wait()
    for copy in copies:
        copy.wait()


def back(o, inner):
    dma = pltpu.SemaphoreType.DMA
    return pl.pallas_call(
        functools.partial(back_kernel, o.shape[0], inner),
        in_specs=[ANY],
        out_specs=ANY,
        out_shape=jax.ShapeDtypeStruct(o.shape, jnp.bfloat16),
        scratch_shapes=[dma((3,)), dma((3,)), dma((1,))],
        compiler_params=pltpu.CompilerParams(collective_id=2, has_side_effects=True),
    )(o)


def attend_kernel(len_ref, q_ref, kv_ref, text_ref, out_ref):
    zq, rows, _ = q_ref.shape
    q = q_ref[...].reshape(zq * rows, HD)
    nt = (((1,), (1,)), ((), ()))
    text = text_ref.shape[1]
    ones = jnp.ones((text, HD), jnp.bfloat16)
    st = lax.dot_general(q, text_ref[0], nt, preferred_element_type=jnp.float32)
    ok = lax.broadcasted_iota(jnp.int32, st.shape, 1) < len_ref[0]
    st = jnp.where(ok, st, -1e30)
    top = jnp.maximum(jnp.max(st, axis=-1, keepdims=True), 0.0)
    pt = jnp.exp2(st - top).astype(jnp.bfloat16)
    acc_t = jnp.dot(
        pt, jnp.concatenate([text_ref[1], ones], axis=1), preferred_element_type=jnp.float32
    )
    _, groups, inner, keys, _ = kv_ref.shape
    ones = jnp.ones((2 * keys, HD), jnp.bfloat16)
    acc = jnp.zeros((zq * rows, 2 * HD), jnp.float32)
    for g in range(groups):
        for i in range(0, inner, 2):
            k = kv_ref[0, g, i : i + 2].reshape(2 * keys, HD)
            v = kv_ref[1, g, i : i + 2].reshape(2 * keys, HD)
            s = lax.dot_general(q, k, nt, preferred_element_type=jnp.float32)
            p = jnp.exp2(s).astype(jnp.bfloat16)
            acc += jnp.dot(
                p, jnp.concatenate([v, ones], axis=1), preferred_element_type=jnp.float32
            )
    acc = acc * jnp.exp2(-top) + acc_t
    out = acc[:, :HD] / acc[:, HD:]
    out_ref[...] = out.astype(jnp.bfloat16).reshape(zq, rows, HD)


def attend(text_len, q_all, kv_all, text):
    qg, rows, width = q_all.shape
    _, groups, inner, keys, _ = kv_all.shape
    step = 2 if qg % 2 == 0 else 1
    return pl.pallas_call(
        attend_kernel,
        grid=(width // HD, qg // step),
        in_specs=[
            pl.BlockSpec(memory_space=pltpu.SMEM),
            pl.BlockSpec((step, rows, HD), lambda h, b: (b, 0, h)),
            pl.BlockSpec((2, groups, inner, keys, HD), lambda h, b: (0, 0, 0, 0, h)),
            pl.BlockSpec((2, text.shape[1], HD), lambda h, b: (0, 0, h)),
        ],
        out_specs=pl.BlockSpec((step, rows, HD), lambda h, b: (b, 0, h)),
        out_shape=jax.ShapeDtypeStruct(q_all.shape, jnp.bfloat16),
        compiler_params=pltpu.CompilerParams(vmem_limit_bytes=48 << 20),
    )(text_len, q_all, kv_all, text)


def total_kernel(sizes, in_ref, out_ref, held, ss, rs):
    places = []
    for axis, size in sizes:
        me = lax.axis_index(axis)
        bit = 1
        while bit < size:
            low = lax.rem(me // bit, 2)
            places.append((axis, me + bit - 2 * bit * low))
            bit *= 2
    barrier = pltpu.get_barrier_semaphore()
    for axis, peer in places:
        pl.semaphore_signal(barrier, inc=1, device_id={axis: peer}, device_id_type=MESH)
    pl.semaphore_wait(barrier, len(places))
    out_ref[...] = in_ref[...]
    for n, (axis, peer) in enumerate(places):
        held[n, 0] = out_ref[...]
        copy = pltpu.make_async_remote_copy(
            src_ref=held.at[n, 0], dst_ref=held.at[n, 1], send_sem=ss.at[n], recv_sem=rs.at[n],
            device_id={axis: peer}, device_id_type=MESH,
        )
        copy.start()
        copy.wait()
        out_ref[...] = held[n, 0] + held[n, 1]


def total(value):
    sizes = (("seq", lax.axis_size("seq")), ("tp", lax.axis_size("tp")))
    steps = sum(size.bit_length() - 1 for _, size in sizes)
    dma = pltpu.SemaphoreType.DMA
    vmem = pl.BlockSpec(memory_space=pltpu.VMEM)
    full = jnp.broadcast_to(value, (8, 128))
    return pl.pallas_call(
        functools.partial(total_kernel, sizes),
        in_specs=[vmem],
        out_specs=vmem,
        out_shape=jax.ShapeDtypeStruct((8, 128), jnp.float32),
        scratch_shapes=[pltpu.VMEM((steps, 2, 8, 128), jnp.float32), dma((steps,)), dma((steps,))],
        compiler_params=pltpu.CompilerParams(collective_id=3, has_side_effects=True),
    )(full)[0, 0]


def shards(latents, noise, timestep, text_len, text_kv, norm_gain, w_qkv, qk_gain, w_out, out_gate):
    rows, local_width = latents.shape
    seq, tp = lax.axis_size("seq"), lax.axis_size("tp")
    at_seq, at_tp = lax.axis_index("seq"), lax.axis_index("tp")
    head_width = w_qkv.shape[2]
    heads_dev = head_width // HD
    groups = 4 if seq == 16 and heads_dev % 4 == 0 else 1
    inner = seq // groups
    width = head_width // groups

    sigma = timestep[0].astype(jnp.float32) / 1000.0
    noisy = (1.0 - sigma) * latents.astype(jnp.float32) + sigma * noise.astype(jnp.float32)
    sent = noisy.astype(jnp.bfloat16)
    if tp == 2:
        other = lax.ppermute(sent, "tp", [(0, 1), (1, 0)])
        first = jnp.where(at_tp == 0, sent, other)
        second = jnp.where(at_tp == 0, other, sent)
        full = jnp.concatenate([first, second], axis=1).astype(jnp.float32)
    else:
        full = lax.all_gather(sent, "tp", axis=1, tiled=True).astype(jnp.float32)
    center = full - jnp.mean(full, axis=-1, keepdims=True)
    spread = jnp.mean(center * center, axis=-1, keepdims=True)
    normed = (center * lax.rsqrt(spread + 1e-06) * norm_gain).astype(jnp.bfloat16)
    gains = jnp.stack(
        [qk_gain[0] * (LOG2E / HD**0.5), qk_gain[1], jnp.ones_like(qk_gain[0])]
    ).reshape(3, 1, HD)
    qkv = project(normed, jnp.transpose(w_qkv, (1, 0, 2)), gains, groups)
    if groups > 1:
        q_all, kv_all = deal(qkv, inner)
        text = lax.dynamic_slice_in_dim(text_kv, (at_seq // inner) * width, width, 2)
        attended = back(attend(text_len, q_all, kv_all, text), inner)
        attended = jnp.transpose(attended, (1, 0, 2)).reshape(rows, head_width)
    else:
        kv_all = lax.all_gather(qkv[1:, 0], "seq", axis=1)[:, None]
        attended = attend(text_len, qkv[0], kv_all, text_kv)[0]
    mixed = jnp.dot(attended, w_out, preferred_element_type=jnp.float32)
    if tp == 2:
        away = lax.dynamic_slice_in_dim(mixed, (1 - at_tp) * local_width, local_width, 1)
        away = lax.ppermute(away.astype(jnp.bfloat16), "tp", [(0, 1), (1, 0)])
        here = lax.dynamic_slice_in_dim(mixed, at_tp * local_width, local_width, 1)
        mixed = here + away.astype(jnp.float32)
    else:
        mixed = lax.psum_scatter(
            mixed.astype(jnp.bfloat16), "tp", scatter_dimension=1, tiled=True
        ).astype(jnp.float32)
    prediction = (noisy + out_gate * mixed).astype(jnp.bfloat16)
    target = noise.astype(jnp.float32) - latents.astype(jnp.float32)
    error = prediction.astype(jnp.float32) - target
    loss = total(jnp.sum(error * error)) / jnp.float32(rows * seq * local_width * tp)
    return (prediction, loss)


def solution(mesh):
    placed = (
        P("seq", "tp"),
        P("seq", "tp"),
        P(),
        P(),
        P(None, None, "tp"),
        P(),
        P(None, None, "tp"),
        P(),
        P("tp", None),
        P("tp"),
    )
    return jax.shard_map(
        shards, mesh=mesh, in_specs=placed, out_specs=(P("seq", "tp"), P()), check_vma=False
    )
```

time: 380 us -> 205 us (0.54)
  waiting for transfers between devices: 176 us -> 34.4 us
  Pallas kernels: 0 us -> 139 us
  local copies, waits for them, and re-layouts: 67.2 us -> 10 us
  matrix products: 55.7 us -> 5.21 us
  blocking collectives: 39.5 us -> 0 us
  other arithmetic: 22.5 us -> 7.29 us
  between operations: 17.1 us -> 4.01 us
  starting transfers between devices: 0.16 us -> 4.55 us
    all_gather x3 -> x0, waiting for transfers between devices: 149 us -> none  [the longest x1 127 us: shards(): gathered = lax.all_gather(paired, 'seq', axis=1, tiled=True)]
    pallas_call x0 -> x5, Pallas kernels: none -> 139 us  [the longest x1 58.8 us: deal(): pl.pallas_call(functools.partial(deal_kernel, groups, inner), in_specs=[A...]
    dot_general x12 -> x1, matrix products: 55.7 us -> 5.21 us  [shards(): mixed = jnp.dot(attended, w_out, preferred_element_type=jnp.float32)]
    psum x1 -> x0, blocking collectives: 39.5 us -> none  [shards(): total_error = lax.psum(jnp.sum(error * error), ('seq', 'tp'))]
    unnamed x23 -> x20, local copies, waits for them, and re-layouts: 39.7 us -> 5.12 us
    ppermute x0 -> x2, waiting for transfers between devices: none -> 34.4 us  [the longest x1 17.7 us: shards(): away = lax.ppermute(away.astype(jnp.bfloat16), 'tp', [(0, 1), (1, 0)])]
    reduce_scatter x1 -> x0, waiting for transfers between devices: 25.1 us -> none  [shards(): lax.psum_scatter(lax.dot_general(w_out, attended, (((0,), (1,)), ((), ())...]
    slice x6 -> x1, local copies, waits for them, and re-layouts: 14.7 us -> 1.2 us  [total(): pl.pallas_call(functools.partial(total_kernel, sizes), in_specs=[vmem], o...]
  transfers between devices with their start and end apart: 4 -> 2, of which waited for: 3 -> 2; matrix products, arithmetic and copies ran while one was open for 12% -> 0% of each run, Pallas kernels for 0% -> 0%
where the time goes in v1:
time: 205 us
  Pallas kernels  139 us (68%)
  waiting for transfers between devices  34.4 us (17%)
  local copies, waits for them, and re-layouts  10 us (5%)
  other arithmetic  7.29 us (4%)
  matrix products  5.21 us (3%)
  starting transfers between devices  4.55 us (2%)
  between operations  4.01 us (2%)
    pallas_call x1, Pallas kernels, deal(): pl.pallas_call(functools.partial(deal_kernel, groups, inner), in_specs=[A...  58.8 us
    pallas_call x1, Pallas kernels, back(): pl.pallas_call(functools.partial(back_kernel, o.shape[0], inner), in_spec...  24.2 us
    pallas_call x1, Pallas kernels, attend(): pl.pallas_call(attend_kernel, grid=(width // HD, qg // step), in_specs=[p...  19.5 us
    pallas_call x1, Pallas kernels, total(): pl.pallas_call(functools.partial(total_kernel, sizes), in_specs=[vmem], o...  18.3 us
    pallas_call x1, Pallas kernels, project(): pl.pallas_call(project_kernel, grid=(3, groups), in_specs=[pl.BlockSpec((...  18.3 us
    ppermute x1, waiting for transfers between devices, shards(): away = lax.ppermute(away.astype(jnp.bfloat16), 'tp', [(0, 1), (1, 0)])  17.7 us
    ppermute x1, waiting for transfers between devices, shards(): other = lax.ppermute(sent, 'tp', [(0, 1), (1, 0)])  16.7 us
    dot_general x1, matrix products, shards(): mixed = jnp.dot(attended, w_out, preferred_element_type=jnp.float32)  5.21 us
  transfers between devices with their start and end apart: 2, of which 2 were waited for; matrix products, arithmetic and copies ran while one was open for 0% of the time, Pallas kernels for 0%

profile of v1, /device:TPU:0, one launch (start us, length us, event | category | flops | bytes accessed | tf_op | source)
XLA Modules:
  0.0 204.6 jit_solution(17230842522503866163)
XLA Ops:
  1.4 1.7 fusion.9
  3.1 3.0 %collective-permute-start = (bf16[256,1536]{1,0:T(8,128)(2,1)S(1)}, bf16[256,1536]{1,0:T(8,128)(2,1)S(1)}, u32[]{:S(2)}, u32[]{:S(2)}) collective-permute-start(bf16[256,1536]{1,0:T(8,128)(2,1)S(1)} %fusion.9), channel_id=1, source_target_pairs={{0,1},{1,0},{2,3},{3,2},{4,5},{5,4},{6,7},{7,6},{8,9},{9,8},{10,11... | collective-permute-start | bytes 2359304 | tf_op jit(solution)/shard_map/ppermute | solution.py:279
  7.0 16.7 %collective-permute-done = bf16[256,1536]{1,0:T(8,128)(2,1)S(1)} collective-permute-done((bf16[256,1536]{1,0:T(8,128)(2,1)S(1)}, bf16[256,1536]{1,0:T(8,128)(2,1)S(1)}, u32[]{:S(2)}, u32[]{:S(2)}) %collective-permute-start) | collective-permute-done | bytes 786464 | tf_op jit(solution)/shard_map/ppermute | solution.py:279
  23.7 0.1 broadcast_select_fusion.1
  23.8 0.3 convert_reduce_fusion
  24.1 0.6 fusion.2
  24.7 0.7 fusion.4.x_ref
  25.4 18.3 %shard_map.113.qkv = bf16[3,4,256,384]{3,2,1,0:T(8,128)(2,1)S(1)} custom-call(bf16[256,3072]{1,0:T(8,128)(2,1)S(1)} %fusion.4.x_ref, bf16[3,3072,1536]{2,1,0:T(8,128)(2,1)} %bitcast.8, f32[3,1,128]{2,1,0:T(1,128)S(1)} %reshape.29.gain_ref), custom_call_target="tpu_custom_call" | custom-call | tf_op jit(solution)/shard_map/pallas_call | solution.py:30
  43.7 1.4 copy-done.1
  45.1 58.8 %shard_map.114 = (bf16[4,256,384]{2,1,0:T(8,128)(2,1)}, bf16[2,4,4,256,384]{4,3,2,1,0:T(8,128)(2,1)}) custom-call(bf16[3,4,256,384]{3,2,1,0:T(8,128)(2,1)} %copy-done.1), custom_call_target="tpu_custom_call" | custom-call | tf_op jit(solution)/shard_map/pallas_call | solution.py:126
  103.9 1.1 copy-done.3
  105.1 19.5 %shard_map.115.o_ref = bf16[4,256,384]{2,1,0:T(8,128)(2,1)S(1)} custom-call(s32[1]{0:T(128)S(6)} %copy.14.len_ref, bf16[4,256,384]{2,1,0:T(8,128)(2,1)S(1)} %copy-done.3, bf16[2,4,4,256,384]{4,3,2,1,0:T(8,128)(2,1)} %get-tuple-element.5.kv_ref, bf16[2,256,384]{2,1,0:T(8,128)(2,1)S(1)} %constant_dynamic-slice_fusion.text_ref), custom_call_target="tpu_custom_call" | custom-call | tf_op jit(solution)/shard_map/pallas_call | solution.py:209
  124.6 0.9 copy-done.2
  125.5 24.2 %shard_map.116 = bf16[4,256,384]{2,1,0:T(8,128)(2,1)} custom-call(bf16[4,256,384]{2,1,0:T(8,128)(2,1)} %copy-done.2), custom_call_target="tpu_custom_call" | custom-call | tf_op jit(solution)/shard_map/pallas_call | solution.py:164
  149.7 1.4 copy.12
  151.1 5.2 %fusion.10 = f32[256,3072]{1,0:T(8,128)S(1)} fusion(bf16[256,1536]{0,1:T(8,128)(2,1)S(1)} %bitcast.9, bf16[1536,3072]{1,0:T(8,128)(2,1)} %param.18), kind=kOutput, calls=%fused_computation.25 | convolution fusion | flops 2415919104 | bytes 13369344 | tf_op jit(solution)/shard_map/dot_general | solution.py:300
  156.3 1.6 copy-done.4
  158.0 1.0 dynamic-slice_convert_fusion
  159.0 1.5 collective-permute-start.1
  160.5 17.7 %collective-permute-done.1 = bf16[256,1536]{1,0:T(8,128)(2,1)} collective-permute-done((bf16[256,1536]{1,0:T(8,128)(2,1)}, bf16[256,1536]{1,0:T(8,128)(2,1)}, u32[]{:S(2)}, u32[]{:S(2)}) %collective-permute-start.1) | collective-permute-done | bytes 786464 | tf_op jit(solution)/shard_map/ppermute | solution.py:303
  178.2 3.9 %fusion.8 = (f32[]{:T(128)}, bf16[256,1536]{1,0:T(8,128)(2,1)}) fusion(bf16[256,1536]{1,0:T(8,128)(2,1)S(1)} %copy-done.5, bf16[256,1536]{1,0:T(8,128)(2,1)S(1)} %copy-done.6, bf16[256,1536]{1,0:T(8,128)(2,1)} %collective-permute-done.1, f32[256,3072]{1,0:T(8,128)} %copy-done.4, s32[]{:T(128)S(6)} %select_n.31, f32[1536]{0:T(1024)S(1)} %copy-done.8, ...), kind=kLoop, calls=%fused_computation.13 | loop fusion | flops 5898239 | bytes 4724752 | tf_op jit(solution)/shard_map/reduce_sum | solution.py:313
  182.1 1.2 broadcast_in_dim.2.in_ref
  183.3 18.3 %shard_map.117 = f32[8,128]{1,0:T(8,128)} custom-call(f32[8,128]{1,0:T(8,128)} %broadcast_in_dim.2.in_ref), custom_call_target="tpu_custom_call" | custom-call | tf_op jit(solution)/shard_map/pallas_call | solution.py:255
  201.6 1.2 slice.11
  (23 shorter events, 0.3 us)
Async XLA Ops:
  0.6 6.3 %copy-start = (bf16[2,256,1536]{2,1,0:T(8,128)(2,1)S(1)}, bf16[2,256,1536]{2,1,0:T(8,128)(2,1)}, u32[]{:S(2)}) copy-start(bf16[2,256,1536]{2,1,0:T(8,128)(2,1)} %param.14) | copy-start | bytes 4718596
  0.6 5.6 %copy-start.9 = (f32[2,128]{1,0:T(2,128)S(1)}, f32[2,128]{1,0:T(2,128)}, u32[]{:S(2)}) copy-start(f32[2,128]{1,0:T(2,128)} %param.17) | copy-start | bytes 3076
  3.1 20.6 %collective-permute-start = (bf16[256,1536]{1,0:T(8,128)(2,1)S(1)}, bf16[256,1536]{1,0:T(8,128)(2,1)S(1)}, u32[]{:S(2)}, u32[]{:S(2)}) collective-permute-start(bf16[256,1536]{1,0:T(8,128)(2,1)S(1)} %fusion.9), channel_id=1, source_target_pairs={{0,1},{1,0},{2,3},{3,2},{4,5},{5,4},{6,7},{7,6},{8,9},{9,8},{10,11... | collective-permute-start | bytes 2359304 | tf_op jit(solution)/shard_map/ppermute | solution.py:279
  23.8 0.9 copy-start.7
  43.7 1.5 copy-start.1
  103.9 1.1 copy-start.3
  124.6 0.9 copy-start.2
  156.3 1.6 copy-start.4
  158.0 20.2 %copy-start.5 = (bf16[256,1536]{1,0:T(8,128)(2,1)S(1)}, bf16[256,1536]{1,0:T(8,128)(2,1)}, u32[]{:S(2)}) copy-start(bf16[256,1536]{1,0:T(8,128)(2,1)} %param.10) | copy-start | bytes 2359300
  158.0 20.2 %copy-start.6 = (bf16[256,1536]{1,0:T(8,128)(2,1)S(1)}, bf16[256,1536]{1,0:T(8,128)(2,1)}, u32[]{:S(2)}) copy-start(bf16[256,1536]{1,0:T(8,128)(2,1)} %param.11) | copy-start | bytes 2359300
  158.0 20.2 %copy-start.8 = (f32[1536]{0:T(1024)S(1)}, f32[1536]{0:T(1024)}, u32[]{:S(2)}) copy-start(f32[1536]{0:T(1024)} %param.19) | copy-start | bytes 18436
  159.0 19.2 %collective-permute-start.1 = (bf16[256,1536]{1,0:T(8,128)(2,1)}, bf16[256,1536]{1,0:T(8,128)(2,1)}, u32[]{:S(2)}, u32[]{:S(2)}) collective-permute-start(bf16[256,1536]{1,0:T(8,128)(2,1)} %dynamic-slice_convert_fusion), channel_id=1, source_target_pairs={{0,1},{1,0},{2,3},{3,2},{4,5},{5,4},{6,7},{7,6},{8,9},{9,8},{10,11... | collective-permute-start | bytes 2359304 | tf_op jit(solution)/shard_map/ppermute | solution.py:303

commit v2 on v1

--- a/solution.py
+++ b/solution.py
@@ -55,7 +55,21 @@
     )
 
 
-def deal_kernel(groups, inner, qkv, q_all, kv_all, zs, zr, qs, qr, xs, xr, cs, cr, fs, fr, ls):
+def group_at(i):
+    return jnp.where(i == 3, 3, lax.rem(i + 1, 3))
+
+
+def tile_at(t):
+    keyed = t < 8
+    return jnp.where(keyed, 1 + lax.rem(t, 2), 0), group_at(jnp.where(keyed, t // 2, t - 8))
+
+
+def deal_kernel(
+    groups, inner, x_ref, w_ref, gain_ref, q_all, kv_all,
+    stage, zs, zr, xs, xr, cs, cr, fs, fr, ls,
+):
+    t = pl.program_id(0)
+    part, to = tile_at(t)
     me = lax.axis_index("seq")
     j = lax.rem(me, inner)
     z = me // inner
@@ -65,113 +79,118 @@
     cj = x * 2 + (1 - core)
     x_mate = z * inner + xj
     c_mate = z * inner + cj
-    order = [2, 1, 3]
-    peers = {k: lax.rem(z + k, groups) * inner + j for k in order}
-    greet([peers[k] for k in order] + [x_mate, c_mate])
-    waits = []
-    firsts = {}
-    for k in order:
-        to = lax.rem(z + k, groups)
-        firsts[k] = remote(
-            qkv.at[pl.ds(1, 2), to], kv_all.at[:, z, j], zs.at[k - 1], zr.at[k - 1], peers[k]
+
+    @pl.when(t == 0)
+    def _():
+        greet([lax.rem(z + k, groups) * inner + j for k in range(1, groups)] + [x_mate, c_mate])
+
+    y = jnp.dot(x_ref[...], w_ref[0], preferred_element_type=jnp.float32)
+    gain = gain_ref[0]
+    for h in range(y.shape[1] // HD):
+        block = y[:, h * HD : (h + 1) * HD]
+        scale = lax.rsqrt(jnp.mean(block * block, axis=-1, keepdims=True) + 1e-06)
+        scale = jnp.where(part < 2, scale, 1.0)
+        stage[part, to, :, h * HD : (h + 1) * HD] = (block * scale * gain).astype(jnp.bfloat16)
+
+    def kv_copy(s, g, frm):
+        return remote(
+            stage.at[s, g], kv_all.at[s - 1, z if frm is None else frm, j], zs.at[s, g],
+            zr.at[s, z if frm is None else frm], g * inner + j,
         )
-        firsts[k].start()
-    own_kv = pltpu.make_async_copy(qkv.at[pl.ds(1, 2), z], kv_all.at[:, z, j], ls.at[0])
-    own_q = pltpu.make_async_copy(qkv.at[0, z], q_all.at[z], ls.at[1])
-    own_kv.start()
-    own_q.start()
-    by_x = {}
-    by_c = {}
-    quers = {}
-    for k in [0] + order:
+
+    def q_copy(g, frm):
+        return remote(
+            stage.at[0, g], q_all.at[z if frm is None else frm], zs.at[0, g],
+            zr.at[0, z if frm is None else frm], g * inner + j,
+        )
+
+    own_kv = pltpu.make_async_copy(stage.at[pl.ds(1, 2), z], kv_all.at[:, z, j], ls.at[0])
+    own_q = pltpu.make_async_copy(stage.at[0, z], q_all.at[z], ls.at[1])
+
+    @pl.when(jnp.logical_and(part > 0, to != z))
+    def _():
+        kv_copy(part, to, None).start()
+
+    @pl.when(jnp.logical_and(part == 0, to != z))
+    def _():
+        q_copy(to, None).start()
+
+    def spread(k):
         at = lax.rem(z + groups - k, groups)
-        if k == 0:
-            src = qkv.at[pl.ds(1, 2), z]
-        else:
-            firsts[k].wait_recv()
-            src = kv_all.at[:, at, j]
-        by_x[k] = remote(src, kv_all.at[:, at, j], xs.at[k], xr.at[k], x_mate)
-        by_x[k].start()
-        by_c[k] = remote(src, kv_all.at[:, at, j], cs.at[k], cr.at[k], c_mate)
-        by_c[k].start()
-        if k == 0:
-            for m in order:
-                to = lax.rem(z + m, groups)
-                quers[m] = remote(
-                    qkv.at[0, to], q_all.at[z], qs.at[m - 1], qr.at[m - 1], peers[m]
-                )
-                quers[m].start()
-    passed = {}
-    for k in [0] + order:
-        at = lax.rem(z + groups - k, groups)
-        by_x[k].wait_recv()
-        passed[k] = remote(
-            kv_all.at[:, at, xj], kv_all.at[:, at, xj], fs.at[k], fr.at[k], c_mate
+        src = stage.at[pl.ds(1, 2), z] if k == 0 else kv_all.at[:, at, j]
+        dst = kv_all.at[:, at, j]
+        return (
+            remote(src, dst, xs.at[k], xr.at[k], x_mate),
+            remote(src, dst, cs.at[k], cr.at[k], c_mate),
         )
-        passed[k].start()
-    own_kv.wait()
-    own_q.wait()
-    for k in order:
-        firsts[k].wait_send()
-        quers[k].wait()
-    for k in [0] + order:
-        by_x[k].wait_send()
-        by_c[k].wait()
-        passed[k].wait()
-
-
-def deal(qkv, inner):
-    _, groups, rows, width = qkv.shape
+
+    @pl.when(t == 7)
+    def _():
+        own_kv.start()
+        for copy in spread(0):
+            copy.start()
+
+    @pl.when(t == 11)
+    def _():
+        own_q.start()
+        order = [1, 3, 2]
+        for k in order:
+            at = lax.rem(z + groups - k, groups)
+            for s in (1, 2):
+                kv_copy(s, at, at).wait_recv()
+            for copy in spread(k):
+                copy.start()
+        passed = []
+        for k in [0] + order:
+            at = lax.rem(z + groups - k, groups)
+            spread(k)[0].wait_recv()
+            slot = kv_all.at[:, at, xj]
+            passed.append(remote(slot, slot, fs.at[k], fr.at[k], c_mate))
+            passed[-1].start()
+        own_kv.wait()
+        own_q.wait()
+        for k in order:
+            at = lax.rem(z + groups - k, groups)
+            for s in (1, 2):
+                kv_copy(s, at, at).wait_send()
+            q_copy(at, at).wait()
+        for k in range(groups):
+            by_x, by_c = spread(k)
+            by_x.wait_send()
+            by_c.wait()
+        for copy in passed:
+            copy.wait()
+
+
+def deal(normed, w, gains, groups, inner):
+    rows, depth = normed.shape
+    width = w.shape[2] // groups
     dma = pltpu.SemaphoreType.DMA
     return pl.pallas_call(
         functools.partial(deal_kernel, groups, inner),
-        in_specs=[ANY],
+        grid=(3 * groups,),
+        in_specs=[
+            pl.BlockSpec((rows, depth), lambda t: (0, 0)),
+            pl.BlockSpec((1, depth, width), lambda t: (tile_at(t)[0], 0, tile_at(t)[1])),
+            pl.BlockSpec((1, 1, HD), lambda t: (tile_at(t)[0], 0, 0)),
+        ],
         out_specs=[ANY, ANY],
         out_shape=[
             jax.ShapeDtypeStruct((groups, rows, width), jnp.bfloat16),
             jax.ShapeDtypeStruct((2, groups, inner, rows, width), jnp.bfloat16),
         ],
-        scratch_shapes=[dma((3,)), dma((3,)), dma((3,)), dma((3,))]
+        scratch_shapes=[
+            pltpu.VMEM((3, groups, rows, width), jnp.bfloat16), dma((3, 4)), dma((3, 4)),
+        ]
         + [dma((4,)) for _ in range(6)]
         + [dma((2,))],
-        compiler_params=pltpu.CompilerParams(collective_id=1, has_side_effects=True),
-    )(qkv)
-
-
-def back_kernel(groups, inner, o_ref, out_ref, ss, rs, ls):
-    me = lax.axis_index("seq")
-    j = lax.rem(me, inner)
-    z = me // inner
-    order = [2, 1, 3]
-    peers = {k: lax.rem(z + k, groups) * inner + j for k in order}
-    greet([peers[k] for k in order])
-    copies = []
-    for k in order:
-        to = lax.rem(z + k, groups)
-        copies.append(
-            remote(o_ref.at[to], out_ref.at[z], ss.at[k - 1], rs.at[k - 1], peers[k])
-        )
-        copies[-1].start()
-    own = pltpu.make_async_copy(o_ref.at[z], out_ref.at[z], ls.at[0])
-    own.start()
-    own.wait()
-    for copy in copies:
-        copy.wait()
-
-
-def back(o, inner):
-    dma = pltpu.SemaphoreType.DMA
-    return pl.pallas_call(
-        functools.partial(back_kernel, o.shape[0], inner),
-        in_specs=[ANY],
-        out_specs=ANY,
-        out_shape=jax.ShapeDtypeStruct(o.shape, jnp.bfloat16),
-        scratch_shapes=[dma((3,)), dma((3,)), dma((1,))],
-        compiler_params=pltpu.CompilerParams(collective_id=2, has_side_effects=True),
-    )(o)
-
-
-def attend_kernel(len_ref, q_ref, kv_ref, text_ref, out_ref):
+        compiler_params=pltpu.CompilerParams(
+            collective_id=1, has_side_effects=True, vmem_limit_bytes=40 << 20
+        ),
+    )(normed, w, gains)
+
+
+def attention(len_ref, q_ref, kv_ref, text_ref):
     zq, rows, _ = q_ref.shape
     q = q_ref[...].reshape(zq * rows, HD)
     nt = (((1,), (1,)), ((), ()))
@@ -199,7 +218,79 @@
             )
     acc = acc * jnp.exp2(-top) + acc_t
     out = acc[:, :HD] / acc[:, HD:]
-    out_ref[...] = out.astype(jnp.bfloat16).reshape(zq, rows, HD)
+    return out.astype(jnp.bfloat16).reshape(zq, rows, HD)
+
+
+def attend_kernel(len_ref, q_ref, kv_ref, text_ref, out_ref):
+    out_ref[...] = attention(len_ref, q_ref, kv_ref, text_ref)
+
+
+def home_kernel(groups, inner, heads, len_ref, q_ref, kv_ref, text_ref, out_ref, stage, ss, rs):
+    h, b = pl.program_id(0), pl.program_id(1)
+    me = lax.axis_index("seq")
+    j = lax.rem(me, inner)
+    z = me // inner
+    zq = q_ref.shape[0]
+
+    @pl.when(jnp.logical_and(h == 0, b == 0))
+    def _():
+        greet([lax.rem(z + k, groups) * inner + j for k in range(1, groups)])
+
+    def columns(frm, head):
+        return out_ref.at[:, pl.ds(pl.multiple_of((frm * heads + head) * HD, HD), HD)]
+
+    out = attention(len_ref, q_ref, kv_ref, text_ref)
+    for n in range(zq):
+        to = b * zq + n
+        stage[to, h] = out[n]
+
+        @pl.when(to != z)
+        def _():
+            remote(
+                stage.at[to, h], columns(z, h), ss.at[to, h], rs.at[z, h], to * inner + j
+            ).start()
+
+        @pl.when(to == z)
+        def _():
+            pltpu.make_async_copy(stage.at[to, h], columns(z, h), ss.at[to, h]).start()
+
+    @pl.when(jnp.logical_and(h == heads - 1, b == groups // zq - 1))
+    def _():
+        for head in range(heads):
+            for k in range(1, groups):
+                at = lax.rem(z + k, groups)
+                remote(
+                    stage.at[at, head], columns(at, head), ss.at[at, head], rs.at[at, head],
+                    at * inner + j,
+                ).wait()
+            pltpu.make_async_copy(stage.at[z, head], columns(z, head), ss.at[z, head]).wait()
+
+
+def attend_home(text_len, q_all, kv_all, text):
+    groups, rows, width = q_all.shape
+    _, _, inner, keys, _ = kv_all.shape
+    heads = width // HD
+    dma = pltpu.SemaphoreType.DMA
+    return pl.pallas_call(
+        functools.partial(home_kernel, groups, inner, heads),
+        grid=(heads, groups // 2),
+        in_specs=[
+            pl.BlockSpec(memory_space=pltpu.SMEM),
+            pl.BlockSpec((2, rows, HD), lambda h, b: (b, 0, h)),
+            pl.BlockSpec((2, groups, inner, keys, HD), lambda h, b: (0, 0, 0, 0, h)),
+            pl.BlockSpec((2, text.shape[1], HD), lambda h, b: (0, 0, h)),
+        ],
+        out_specs=ANY,
+        out_shape=jax.ShapeDtypeStruct((rows, groups * width), jnp.bfloat16),
+        scratch_shapes=[
+            pltpu.VMEM((groups, heads, rows, HD), jnp.bfloat16),
+            dma((groups, heads)),
+            dma((groups, heads)),
+        ],
+        compiler_params=pltpu.CompilerParams(
+            collective_id=2, has_side_effects=True, vmem_limit_bytes=48 << 20
+        ),
+    )(text_len, q_all, kv_all, text)
 
 
 def attend(text_len, q_all, kv_all, text):
@@ -219,6 +310,65 @@
         out_shape=jax.ShapeDtypeStruct(q_all.shape, jnp.bfloat16),
         compiler_params=pltpu.CompilerParams(vmem_limit_bytes=48 << 20),
     )(text_len, q_all, kv_all, text)
+
+
+def pair_kernel(groups, inner, tp, in_ref, out_ref, near, far, ns, nr, fs, fr):
+    me, at_tp = lax.axis_index("seq"), lax.axis_index("tp")
+    z, j = me // inner, lax.rem(me, inner)
+    size = inner * tp
+    slot = at_tp * inner + j
+    peers = []
+    for k in range(1, size):
+        other = lax.rem(slot + k, size)
+        peers.append((other, (z * inner + lax.rem(other, inner), other // inner)))
+    fars = []
+    for k in range(1, groups):
+        other = lax.rem(z + k, groups)
+        fars.append((other, (other * inner + j, at_tp)))
+    barrier = pltpu.get_barrier_semaphore()
+    for _, peer in peers + fars:
+        pl.semaphore_signal(barrier, inc=1, device_id=peer, device_id_type=MESH)
+    pl.semaphore_wait(barrier, len(peers) + len(fars))
+
+    def round_of(held, mine, others, send, recv):
+        copies = []
+        for other, peer in others:
+            copy = pltpu.make_async_remote_copy(
+                src_ref=held.at[mine], dst_ref=held.at[mine], send_sem=send.at[other],
+                recv_sem=recv.at[mine], device_id=peer, device_id_type=MESH,
+            )
+            copy.start()
+        for other, peer in others:
+            copy = pltpu.make_async_remote_copy(
+                src_ref=held.at[other], dst_ref=held.at[other], send_sem=send.at[other],
+                recv_sem=recv.at[other], device_id=peer, device_id_type=MESH,
+            )
+            copy.wait()
+
+    near[slot] = in_ref[...]
+    round_of(near, slot, peers, ns, nr)
+    far[z] = jnp.sum(near[...], axis=0)
+    round_of(far, z, fars, fs, fr)
+    out_ref[...] = jnp.sum(far[...], axis=0)
+
+
+def pair_total(value, groups, inner):
+    tp = lax.axis_size("tp")
+    size = inner * tp
+    dma = pltpu.SemaphoreType.DMA
+    vmem = pl.BlockSpec(memory_space=pltpu.VMEM)
+    return pl.pallas_call(
+        functools.partial(pair_kernel, groups, inner, tp),
+        in_specs=[vmem],
+        out_specs=vmem,
+        out_shape=jax.ShapeDtypeStruct((8, 128), jnp.float32),
+        scratch_shapes=[
+            pltpu.VMEM((size, 8, 128), jnp.float32),
+            pltpu.VMEM((groups, 8, 128), jnp.float32),
+            dma((size,)), dma((size,)), dma((groups,)), dma((groups,)),
+        ],
+        compiler_params=pltpu.CompilerParams(collective_id=4, has_side_effects=True),
+    )(jnp.broadcast_to(value, (8, 128)))[0, 0]
 
 
 def total_kernel(sizes, in_ref, out_ref, held, ss, rs):
@@ -288,13 +438,13 @@
     gains = jnp.stack(
         [qk_gain[0] * (LOG2E / HD**0.5), qk_gain[1], jnp.ones_like(qk_gain[0])]
     ).reshape(3, 1, HD)
-    qkv = project(normed, jnp.transpose(w_qkv, (1, 0, 2)), gains, groups)
+    w = jnp.transpose(w_qkv, (1, 0, 2))
     if groups > 1:
-        q_all, kv_all = deal(qkv, inner)
+        q_all, kv_all = deal(normed, w, gains, groups, inner)
         text = lax.dynamic_slice_in_dim(text_kv, (at_seq // inner) * width, width, 2)
-        attended = back(attend(text_len, q_all, kv_all, text), inner)
-        attended = jnp.transpose(attended, (1, 0, 2)).reshape(rows, head_width)
+        attended = attend_home(text_len, q_all, kv_all, text)
     else:
+        qkv = project(normed, w, gains, groups)
         kv_all = lax.all_gather(qkv[1:, 0], "seq", axis=1)[:, None]
         attended = attend(text_len, qkv[0], kv_all, text_kv)[0]
     mixed = jnp.dot(attended, w_out, preferred_element_type=jnp.float32)
@@ -310,7 +460,9 @@
     prediction = (noisy + out_gate * mixed).astype(jnp.bfloat16)
     target = noise.astype(jnp.float32) - latents.astype(jnp.float32)
     error = prediction.astype(jnp.float32) - target
-    loss = total(jnp.sum(error * error)) / jnp.float32(rows * seq * local_width * tp)
+    squares = jnp.sum(error * error)
+    summed = pair_total(squares, groups, inner) if groups > 1 else total(squares)
+    loss = summed / jnp.float32(rows * seq * local_width * tp)
     return (prediction, loss)
 
 

time: 205 us -> 164 us (0.80)
  Pallas kernels: 139 us -> 103 us
  matrix products: 5.21 us -> 2.6 us
  local copies, waits for them, and re-layouts: 10 us -> 7.81 us
    pallas_call x5 -> x3, Pallas kernels: 139 us -> 103 us  [the longest x1 62.4 us: deal(): pl.pallas_call(functools.partial(deal_kernel, groups, inner), grid=(3 * g...]
    dot_general x1, matrix products: 5.21 us -> 2.6 us  [shards(): mixed = jnp.dot(attended, w_out, preferred_element_type=jnp.float32)]
    unnamed x20 -> x22, local copies, waits for them, and re-layouts: 5.12 us -> 4.32 us
where the time goes in v2:
time: 164 us; the launch traced here: 163 us
  Pallas kernels  103 us (63%)
  waiting for transfers between devices  34.5 us (21%)
  local copies, waits for them, and re-layouts  7.81 us (5%)
  other arithmetic  7.26 us (4%)
  starting transfers between devices  4.55 us (3%)
  between operations  4.02 us (2%)
  matrix products  2.6 us (2%)
    pallas_call x1, Pallas kernels, deal(): pl.pallas_call(functools.partial(deal_kernel, groups, inner), grid=(3 * g...  62.4 us
    pallas_call x1, Pallas kernels, attend_home(): pl.pallas_call(functools.partial(home_kernel, groups, inner, heads), grid...  26.4 us
    ppermute x1, waiting for transfers between devices, shards(): away = lax.ppermute(away.astype(jnp.bfloat16), 'tp', [(0, 1), (1, 0)])  17.8 us
    ppermute x1, waiting for transfers between devices, shards(): other = lax.ppermute(sent, 'tp', [(0, 1), (1, 0)])  16.7 us
    pallas_call x1, Pallas kernels, pair_total(): pl.pallas_call(functools.partial(pair_kernel, groups, inner, tp), in_spec...  13.9 us
    unnamed x22, local copies, waits for them, and re-layouts  4.32 us
    reduce_sum x1, other arithmetic, shards(): squares = jnp.sum(error * error)  3.88 us
  transfers between devices with their start and end apart: 2, of which 2 were waited for; matrix products, arithmetic and copies ran while one was open for 0% of the time, Pallas kernels for 0%

profile of v2, /device:TPU:0, one launch (start us, length us, event | category | flops | bytes accessed | tf_op | source)
XLA Modules:
  0.0 163.3 jit_solution(14642337729355360227)
XLA Ops:
  0.6 0.0 copy-start
  1.4 1.7 %fusion.9 = bf16[256,1536]{1,0:T(8,128)(2,1)S(1)} fusion(bf16[256,1536]{1,0:T(8,128)(2,1)} %param.11, bf16[256,1536]{1,0:T(8,128)(2,1)} %param.10, f32[]{:T(128)} %bitcast, f32[]{:T(128)S(6)} %sub.24), kind=kLoop, calls=%fused_computation.17 | loop fusion | flops 2359296 | bytes 2359304 | tf_op jit(solution)/shard_map/convert_element_type | solution.py:427
  3.1 3.0 %collective-permute-start = (bf16[256,1536]{1,0:T(8,128)(2,1)S(1)}, bf16[256,1536]{1,0:T(8,128)(2,1)S(1)}, u32[]{:S(2)}, u32[]{:S(2)}) collective-permute-start(bf16[256,1536]{1,0:T(8,128)(2,1)S(1)} %fusion.9), channel_id=1, source_target_pairs={{0,1},{1,0},{2,3},{3,2},{4,5},{5,4},{6,7},{7,6},{8,9},{9,8},{10,11... | collective-permute-start | bytes 2359304 | tf_op jit(solution)/shard_map/ppermute | solution.py:429
  6.1 0.1 pad.2.clone
  6.2 0.1 maximum_maximum_fusion
  7.0 16.7 %collective-permute-done = bf16[256,1536]{1,0:T(8,128)(2,1)S(1)} collective-permute-done((bf16[256,1536]{1,0:T(8,128)(2,1)S(1)}, bf16[256,1536]{1,0:T(8,128)(2,1)S(1)}, u32[]{:S(2)}, u32[]{:S(2)}) %collective-permute-start) | collective-permute-done | bytes 786464 | tf_op jit(solution)/shard_map/ppermute | solution.py:429
  23.7 0.1 broadcast_select_fusion.1
  23.8 0.3 convert_reduce_fusion
  24.1 0.6 fusion.2
  24.7 0.0 slice-start
  24.7 0.7 fusion.4.x_ref
  25.4 0.0 slice-start.1
  25.4 62.4 %shard_map.113 = (bf16[4,256,384]{2,1,0:T(8,128)(2,1)S(1)}, bf16[2,4,4,256,384]{4,3,2,1,0:T(8,128)(2,1)S(1)}) custom-call(bf16[256,3072]{1,0:T(8,128)(2,1)S(1)} %fusion.4.x_ref, bf16[3,3072,1536]{2,1,0:T(8,128)(2,1)} %bitcast.6, f32[3,1,128]{2,1,0:T(1,128)S(1)} %reshape.26.gain_ref), custom_call_target="tpu_custom_call" | custom-call | tf_op jit(solution)/shard_map/pallas_call | solution.py:169
  87.8 2.6 %copy-done.1 = bf16[2,4,4,256,384]{4,3,2,1,0:T(8,128)(2,1)} copy-done((bf16[2,4,4,256,384]{4,3,2,1,0:T(8,128)(2,1)}, bf16[2,4,4,256,384]{4,3,2,1,0:T(8,128)(2,1)S(1)}, u32[]{:S(2)}) %copy-start.1) | copy-done | bytes 6291480
  90.4 26.4 %shard_map.114 = bf16[256,1536]{1,0:T(8,128)(2,1)S(1)} custom-call(s32[1]{0:T(128)S(6)} %copy.13.len_ref, bf16[4,256,384]{2,1,0:T(8,128)(2,1)S(1)} %get-tuple-element.4.q_ref, bf16[2,4,4,256,384]{4,3,2,1,0:T(8,128)(2,1)} %copy-done.1, bf16[2,256,384]{2,1,0:T(8,128)(2,1)S(1)} %constant_dynamic-slice_fusion.text_ref), custom_call_target="tpu_custom_call" | custom-call | tf_op jit(solution)/shard_map/pallas_call | solution.py:274
  116.9 2.6 %fusion.10 = f32[256,3072]{1,0:T(8,128)S(1)} fusion(bf16[256,1536]{1,0:T(8,128)(2,1)S(1)} %shard_map.114, bf16[1536,3072]{1,0:T(8,128)(2,1)S(1)} %bitcast.8), kind=kOutput, calls=%fused_computation.25 | convolution fusion | flops 2415919104 | bytes 13369344 | tf_op jit(solution)/shard_map/dot_general | solution.py:450
  119.5 1.6 copy-done.4
  121.1 1.0 dynamic-slice_convert_fusion
  122.1 1.5 collective-permute-start.1
  123.6 17.8 %collective-permute-done.1 = bf16[256,1536]{1,0:T(8,128)(2,1)} collective-permute-done((bf16[256,1536]{1,0:T(8,128)(2,1)}, bf16[256,1536]{1,0:T(8,128)(2,1)}, u32[]{:S(2)}, u32[]{:S(2)}) %collective-permute-start.1) | collective-permute-done | bytes 786464 | tf_op jit(solution)/shard_map/ppermute | solution.py:453
  141.4 3.9 %fusion.8 = (f32[]{:T(128)}, bf16[256,1536]{1,0:T(8,128)(2,1)}) fusion(bf16[256,1536]{1,0:T(8,128)(2,1)S(1)} %copy-done.2, bf16[256,1536]{1,0:T(8,128)(2,1)S(1)} %copy-done.3, bf16[256,1536]{1,0:T(8,128)(2,1)} %collective-permute-done.1, f32[256,3072]{1,0:T(8,128)} %copy-done.4, s32[]{:T(128)S(6)} %select_n.31, f32[1536]{0:T(1024)S(1)} %copy-done.6, ...), kind=kLoop, calls=%fused_computation.13 | loop fusion | flops 5898239 | bytes 4724752 | tf_op jit(solution)/shard_map/reduce_sum | solution.py:463
  145.3 1.2 broadcast_in_dim.2.in_ref
  146.5 13.9 %shard_map.115 = f32[8,128]{1,0:T(8,128)} custom-call(f32[8,128]{1,0:T(8,128)} %broadcast_in_dim.2.in_ref), custom_call_target="tpu_custom_call" | custom-call | tf_op jit(solution)/shard_map/pallas_call | solution.py:360
  160.4 1.2 slice.11
  (23 shorter events, 0.1 us)
Async XLA Ops:
  0.6 6.3 %copy-start = (bf16[2,256,1536]{2,1,0:T(8,128)(2,1)S(1)}, bf16[2,256,1536]{2,1,0:T(8,128)(2,1)}, u32[]{:S(2)}) copy-start(bf16[2,256,1536]{2,1,0:T(8,128)(2,1)} %param.14) | copy-start | bytes 4718596
  0.6 5.6 %copy-start.7 = (f32[2,128]{1,0:T(2,128)S(1)}, f32[2,128]{1,0:T(2,128)}, u32[]{:S(2)}) copy-start(f32[2,128]{1,0:T(2,128)} %param.17) | copy-start | bytes 3076
  3.1 20.6 %collective-permute-start = (bf16[256,1536]{1,0:T(8,128)(2,1)S(1)}, bf16[256,1536]{1,0:T(8,128)(2,1)S(1)}, u32[]{:S(2)}, u32[]{:S(2)}) collective-permute-start(bf16[256,1536]{1,0:T(8,128)(2,1)S(1)} %fusion.9), channel_id=1, source_target_pairs={{0,1},{1,0},{2,3},{3,2},{4,5},{5,4},{6,7},{7,6},{8,9},{9,8},{10,11... | collective-permute-start | bytes 2359304 | tf_op jit(solution)/shard_map/ppermute | solution.py:429
  23.8 0.9 copy-start.5
  24.7 92.2 %slice-start = ((s8[9437184]{0:T(1024)(128)(4,1)}), s8[1048576]{0:T(1024)(128)(4,1)S(1)}, s32[]{:S(2)}) async-start(s8[9437184]{0:T(1024)(128)(4,1)} %bitcast.7), calls=%async_computation | async-start | bytes 2097152
  25.4 91.5 %slice-start.1 = ((s8[9437184]{0:T(1024)(128)(4,1)}), s8[4194304]{0:T(1024)(128)(4,1)S(1)}, s32[]{:S(2)}) async-start(s8[9437184]{0:T(1024)(128)(4,1)} %bitcast.7), calls=%async_computation.1 | async-start | bytes 8388608
  25.4 91.5 %slice-start.2 = ((s8[9437184]{0:T(1024)(128)(4,1)}), s8[4194304]{0:T(1024)(128)(4,1)S(1)}, s32[]{:S(2)}) async-start(s8[9437184]{0:T(1024)(128)(4,1)} %bitcast.7), calls=%async_computation.2 | async-start | bytes 8388608
  87.8 2.7 %copy-start.1 = (bf16[2,4,4,256,384]{4,3,2,1,0:T(8,128)(2,1)}, bf16[2,4,4,256,384]{4,3,2,1,0:T(8,128)(2,1)S(1)}, u32[]{:S(2)}) copy-start(bf16[2,4,4,256,384]{4,3,2,1,0:T(8,128)(2,1)S(1)} %get-tuple-element.5.kv_ref) | copy-start | bytes 18874372
  119.5 1.6 copy-start.4
  121.1 20.3 %copy-start.2 = (bf16[256,1536]{1,0:T(8,128)(2,1)S(1)}, bf16[256,1536]{1,0:T(8,128)(2,1)}, u32[]{:S(2)}) copy-start(bf16[256,1536]{1,0:T(8,128)(2,1)} %param.10) | copy-start | bytes 2359300
  121.1 20.3 %copy-start.3 = (bf16[256,1536]{1,0:T(8,128)(2,1)S(1)}, bf16[256,1536]{1,0:T(8,128)(2,1)}, u32[]{:S(2)}) copy-start(bf16[256,1536]{1,0:T(8,128)(2,1)} %param.11) | copy-start | bytes 2359300
  121.1 20.3 %copy-start.6 = (f32[1536]{0:T(1024)S(1)}, f32[1536]{0:T(1024)}, u32[]{:S(2)}) copy-start(f32[1536]{0:T(1024)} %param.19) | copy-start | bytes 18436
  122.1 19.3 %collective-permute-start.1 = (bf16[256,1536]{1,0:T(8,128)(2,1)}, bf16[256,1536]{1,0:T(8,128)(2,1)}, u32[]{:S(2)}, u32[]{:S(2)}) collective-permute-start(bf16[256,1536]{1,0:T(8,128)(2,1)} %dynamic-slice_convert_fusion), channel_id=1, source_target_pairs={{0,1},{1,0},{2,3},{3,2},{4,5},{5,4},{6,7},{7,6},{8,9},{9,8},{10,11... | collective-permute-start | bytes 2359304 | tf_op jit(solution)/shard_map/ppermute | solution.py:453

commit v3 on v2

--- a/solution.py
+++ b/solution.py
@@ -447,13 +447,18 @@
         qkv = project(normed, w, gains, groups)
         kv_all = lax.all_gather(qkv[1:, 0], "seq", axis=1)[:, None]
         attended = attend(text_len, qkv[0], kv_all, text_kv)[0]
-    mixed = jnp.dot(attended, w_out, preferred_element_type=jnp.float32)
     if tp == 2:
-        away = lax.dynamic_slice_in_dim(mixed, (1 - at_tp) * local_width, local_width, 1)
-        away = lax.ppermute(away.astype(jnp.bfloat16), "tp", [(0, 1), (1, 0)])
-        here = lax.dynamic_slice_in_dim(mixed, at_tp * local_width, local_width, 1)
-        mixed = here + away.astype(jnp.float32)
+        half = rows // 2
+        parts = []
+        for at in (0, half):
+            part = jnp.dot(attended[at : at + half], w_out, preferred_element_type=jnp.float32)
+            low, high = part[:, :local_width], part[:, local_width:]
+            away = jnp.where(at_tp == 0, high, low).astype(jnp.bfloat16)
+            away = lax.ppermute(away, "tp", [(0, 1), (1, 0)])
+            parts.append(jnp.where(at_tp == 0, low, high) + away.astype(jnp.float32))
+        mixed = jnp.concatenate(parts, axis=0)
     else:
+        mixed = jnp.dot(attended, w_out, preferred_element_type=jnp.float32)
         mixed = lax.psum_scatter(
             mixed.astype(jnp.bfloat16), "tp", scatter_dimension=1, tiled=True
         ).astype(jnp.float32)

time: 164 us -> 160 us (0.976)
  local copies, waits for them, and re-layouts: 7.81 us -> 5.24 us
    reduce_sum x1, other arithmetic: 3.88 us -> 2.09 us  [shards(): squares = jnp.sum(error * error)]
    unnamed x22 -> x20, local copies, waits for them, and re-layouts: 4.32 us -> 2.71 us
    ppermute x1 -> x2, waiting for transfers between devices: 17.8 us -> 16.7 us  [shards(): away = lax.ppermute(away, 'tp', [(0, 1), (1, 0)])]
  transfers between devices with their start and end apart: 2 -> 3, of which waited for: 2 -> 3; matrix products, arithmetic and copies ran while one was open for 0% -> 0% of each run, Pallas kernels for 0% -> 0%
where the time goes in v3:
time: 160 us; the launch traced here: 159 us
  Pallas kernels  103 us (64%)
  waiting for transfers between devices  33.3 us (21%)
  other arithmetic  5.88 us (4%)
  local copies, waits for them, and re-layouts  5.24 us (3%)
  starting transfers between devices  5.19 us (3%)
  between operations  4.09 us (3%)
  matrix products  2.78 us (2%)
    pallas_call x1, Pallas kernels, deal(): pl.pallas_call(functools.partial(deal_kernel, groups, inner), grid=(3 * g...  62.6 us
    pallas_call x1, Pallas kernels, attend_home(): pl.pallas_call(functools.partial(home_kernel, groups, inner, heads), grid...  26.4 us
    ppermute x2, waiting for transfers between devices, shards(): away = lax.ppermute(away, 'tp', [(0, 1), (1, 0)])  16.7 us
    ppermute x1, waiting for transfers between devices, shards(): other = lax.ppermute(sent, 'tp', [(0, 1), (1, 0)])  16.7 us
    pallas_call x1, Pallas kernels, pair_total(): pl.pallas_call(functools.partial(pair_kernel, groups, inner, tp), in_spec...  13.9 us
  transfers between devices with their start and end apart: 3, of which 3 were waited for; matrix products, arithmetic and copies ran while one was open for 0% of the time, Pallas kernels for 0%

profile of v3, /device:TPU:0, one launch (start us, length us, event | category | flops | bytes accessed | tf_op | source)
XLA Modules:
  0.0 159.4 jit_solution(4857372557812016031)
XLA Ops:
  1.4 1.7 %fusion.11 = bf16[256,1536]{1,0:T(8,128)(2,1)S(1)} fusion(bf16[256,1536]{1,0:T(8,128)(2,1)} %param.11, bf16[256,1536]{1,0:T(8,128)(2,1)} %param.10, f32[]{:T(128)} %bitcast, f32[]{:T(128)S(6)} %sub.21), kind=kLoop, calls=%fused_computation.18 | loop fusion | flops 2359296 | bytes 2359304 | tf_op jit(solution)/shard_map/convert_element_type | solution.py:427
  3.1 3.0 %collective-permute-start = (bf16[256,1536]{1,0:T(8,128)(2,1)S(1)}, bf16[256,1536]{1,0:T(8,128)(2,1)S(1)}, u32[]{:S(2)}, u32[]{:S(2)}) collective-permute-start(bf16[256,1536]{1,0:T(8,128)(2,1)S(1)} %fusion.11), channel_id=1, source_target_pairs={{0,1},{1,0},{2,3},{3,2},{4,5},{5,4},{6,7},{7,6},{8,9},{9,8},{10,11... | collective-permute-start | bytes 2359304 | tf_op jit(solution)/shard_map/ppermute | solution.py:429
  6.1 0.1 pad.4.clone
  6.2 0.1 maximum_maximum_fusion
  7.0 16.7 %collective-permute-done = bf16[256,1536]{1,0:T(8,128)(2,1)S(1)} collective-permute-done((bf16[256,1536]{1,0:T(8,128)(2,1)S(1)}, bf16[256,1536]{1,0:T(8,128)(2,1)S(1)}, u32[]{:S(2)}, u32[]{:S(2)}) %collective-permute-start) | collective-permute-done | bytes 786464 | tf_op jit(solution)/shard_map/ppermute | solution.py:429
  23.7 0.1 broadcast_select_fusion.1
  23.8 0.3 convert_reduce_fusion
  24.1 0.6 fusion.2
  24.7 0.7 fusion.4.x_ref
  25.4 62.6 %shard_map.113 = (bf16[4,256,384]{2,1,0:T(8,128)(2,1)S(1)}, bf16[2,4,4,256,384]{4,3,2,1,0:T(8,128)(2,1)S(1)}) custom-call(bf16[256,3072]{1,0:T(8,128)(2,1)S(1)} %fusion.4.x_ref, bf16[3,3072,1536]{2,1,0:T(8,128)(2,1)} %bitcast.8, f32[3,1,128]{2,1,0:T(1,128)S(1)} %reshape.26.gain_ref), custom_call_target="tpu_custom_call" | custom-call | tf_op jit(solution)/shard_map/pallas_call | solution.py:169
  88.0 2.6 %copy-done.1 = bf16[2,4,4,256,384]{4,3,2,1,0:T(8,128)(2,1)} copy-done((bf16[2,4,4,256,384]{4,3,2,1,0:T(8,128)(2,1)}, bf16[2,4,4,256,384]{4,3,2,1,0:T(8,128)(2,1)S(1)}, u32[]{:S(2)}) %copy-start.1) | copy-done | bytes 6291480
  90.7 26.4 %shard_map.114 = bf16[256,1536]{1,0:T(8,128)(2,1)S(1)} custom-call(s32[1]{0:T(128)S(6)} %copy.13.len_ref, bf16[4,256,384]{2,1,0:T(8,128)(2,1)S(1)} %get-tuple-element.4.q_ref, bf16[2,4,4,256,384]{4,3,2,1,0:T(8,128)(2,1)} %copy-done.1, bf16[2,256,384]{2,1,0:T(8,128)(2,1)S(1)} %constant_dynamic-slice_fusion.text_ref), custom_call_target="tpu_custom_call" | custom-call | tf_op jit(solution)/shard_map/pallas_call | solution.py:274
  117.1 1.4 fusion.14
  118.5 1.4 fusion.12
  120.0 1.6 collective-permute-start.1
  121.6 0.6 collective-permute-start.2
  122.2 9.9 %collective-permute-done.1 = bf16[128,1536]{1,0:T(8,128)(2,1)S(1)} collective-permute-done((bf16[128,1536]{1,0:T(8,128)(2,1)S(1)}, bf16[128,1536]{1,0:T(8,128)(2,1)S(1)}, u32[]{:S(2)}, u32[]{:S(2)}) %collective-permute-start.1) | collective-permute-done | bytes 393248 | tf_op jit(solution)/shard_map/ppermute | solution.py:457
  132.1 0.1 convert_add_fusion.1
  132.3 6.8 %collective-permute-done.2 = bf16[128,1536]{1,0:T(8,128)(2,1)S(1)} collective-permute-done((bf16[128,1536]{1,0:T(8,128)(2,1)S(1)}, bf16[128,1536]{1,0:T(8,128)(2,1)S(1)}, u32[]{:S(2)}, u32[]{:S(2)}) %collective-permute-start.2) | collective-permute-done | bytes 393248 | tf_op jit(solution)/shard_map/ppermute | solution.py:457
  139.0 0.1 convert_add_fusion
  139.2 2.1 %fusion.8 = (f32[]{:T(128)}, bf16[256,1536]{1,0:T(8,128)(2,1)}) fusion(bf16[256,1536]{1,0:T(8,128)(2,1)S(1)} %copy-done.2, bf16[256,1536]{1,0:T(8,128)(2,1)S(1)} %copy-done.3, f32[128,1536]{1,0:T(8,128)S(1)} %convert_add_fusion, f32[128,1536]{1,0:T(8,128)S(1)} %convert_add_fusion.1, f32[1536]{0:T(1024)S(1)} %copy-done.5, f32[]{:T(128)} %bitcast, f32[]{:T(128)S(6)} %sub.21), kind=kLoop, calls=%fused_computation.13 | loop fusion | flops 5505023 | bytes 3938316 | tf_op jit(solution)/shard_map/reduce_sum | solution.py:468
  141.3 1.2 broadcast_in_dim.2.in_ref
  142.5 13.9 %shard_map.115 = f32[8,128]{1,0:T(8,128)} custom-call(f32[8,128]{1,0:T(8,128)} %broadcast_in_dim.2.in_ref), custom_call_target="tpu_custom_call" | custom-call | tf_op jit(solution)/shard_map/pallas_call | solution.py:360
  156.4 1.2 slice.35
  (27 shorter events, 0.3 us)
Async XLA Ops:
  0.6 6.3 %copy-start = (bf16[2,256,1536]{2,1,0:T(8,128)(2,1)S(1)}, bf16[2,256,1536]{2,1,0:T(8,128)(2,1)}, u32[]{:S(2)}) copy-start(bf16[2,256,1536]{2,1,0:T(8,128)(2,1)} %param.14) | copy-start | bytes 4718596
  0.6 5.6 %copy-start.6 = (f32[2,128]{1,0:T(2,128)S(1)}, f32[2,128]{1,0:T(2,128)}, u32[]{:S(2)}) copy-start(f32[2,128]{1,0:T(2,128)} %param.17) | copy-start | bytes 3076
  3.1 20.6 %collective-permute-start = (bf16[256,1536]{1,0:T(8,128)(2,1)S(1)}, bf16[256,1536]{1,0:T(8,128)(2,1)S(1)}, u32[]{:S(2)}, u32[]{:S(2)}) collective-permute-start(bf16[256,1536]{1,0:T(8,128)(2,1)S(1)} %fusion.11), channel_id=1, source_target_pairs={{0,1},{1,0},{2,3},{3,2},{4,5},{5,4},{6,7},{7,6},{8,9},{9,8},{10,11... | collective-permute-start | bytes 2359304 | tf_op jit(solution)/shard_map/ppermute | solution.py:429
  23.8 0.9 copy-start.4
  24.7 92.4 %slice-start = ((s8[9437184]{0:T(1024)(128)(4,1)}), s8[4194304]{0:T(1024)(128)(4,1)S(1)}, s32[]{:S(2)}) async-start(s8[9437184]{0:T(1024)(128)(4,1)} %bitcast.6), calls=%async_computation | async-start | bytes 8388608
  25.4 91.7 %slice-start.1 = ((s8[9437184]{0:T(1024)(128)(4,1)}), s8[4194304]{0:T(1024)(128)(4,1)S(1)}, s32[]{:S(2)}) async-start(s8[9437184]{0:T(1024)(128)(4,1)} %bitcast.6), calls=%async_computation.1 | async-start | bytes 8388608
  25.4 91.7 %slice-start.2 = ((s8[9437184]{0:T(1024)(128)(4,1)}), s8[1048576]{0:T(1024)(128)(4,1)S(1)}, s32[]{:S(2)}) async-start(s8[9437184]{0:T(1024)(128)(4,1)} %bitcast.6), calls=%async_computation.2 | async-start | bytes 2097152
  88.0 2.7 %copy-start.1 = (bf16[2,4,4,256,384]{4,3,2,1,0:T(8,128)(2,1)}, bf16[2,4,4,256,384]{4,3,2,1,0:T(8,128)(2,1)S(1)}, u32[]{:S(2)}) copy-start(bf16[2,4,4,256,384]{4,3,2,1,0:T(8,128)(2,1)S(1)} %get-tuple-element.5.kv_ref) | copy-start | bytes 18874372
  120.0 12.1 %collective-permute-start.1 = (bf16[128,1536]{1,0:T(8,128)(2,1)S(1)}, bf16[128,1536]{1,0:T(8,128)(2,1)S(1)}, u32[]{:S(2)}, u32[]{:S(2)}) collective-permute-start(bf16[128,1536]{1,0:T(8,128)(2,1)S(1)} %select_convert_fusion.1), channel_id=1, source_target_pairs={{0,1},{1,0},{2,3},{3,2},{4,5},{5,4},{6,7},{7,6},{8,9},{9,8},{10,11... | collective-permute-start | bytes 1179656 | tf_op jit(solution)/shard_map/ppermute | solution.py:457
  121.6 17.4 %collective-permute-start.2 = (bf16[128,1536]{1,0:T(8,128)(2,1)S(1)}, bf16[128,1536]{1,0:T(8,128)(2,1)S(1)}, u32[]{:S(2)}, u32[]{:S(2)}) collective-permute-start(bf16[128,1536]{1,0:T(8,128)(2,1)S(1)} %select_convert_fusion), channel_id=1, source_target_pairs={{0,1},{1,0},{2,3},{3,2},{4,5},{5,4},{6,7},{7,6},{8,9},{9,8},{10,11... | collective-permute-start | bytes 1179656 | tf_op jit(solution)/shard_map/ppermute | solution.py:457
  132.2 7.0 %copy-start.2 = (bf16[256,1536]{1,0:T(8,128)(2,1)S(1)}, bf16[256,1536]{1,0:T(8,128)(2,1)}, u32[]{:S(2)}) copy-start(bf16[256,1536]{1,0:T(8,128)(2,1)} %param.10) | copy-start | bytes 2359300
  132.2 7.0 %copy-start.3 = (bf16[256,1536]{1,0:T(8,128)(2,1)S(1)}, bf16[256,1536]{1,0:T(8,128)(2,1)}, u32[]{:S(2)}) copy-start(bf16[256,1536]{1,0:T(8,128)(2,1)} %param.11) | copy-start | bytes 2359300
  132.2 7.0 %copy-start.5 = (f32[1536]{0:T(1024)S(1)}, f32[1536]{0:T(1024)}, u32[]{:S(2)}) copy-start(f32[1536]{0:T(1024)} %param.19) | copy-start | bytes 18436
